TPU v7x, 256 devices: a whole 4x4x8 slice. The times are simulated.
256 devices in a mesh: ctx: 64 (over x, y_hi, z), head: 4 (over y_lo, core).
Axes of the slice: x: 4, y: 4 (y_hi: 2, y_lo: 2; y = y_hi * 2 + y_lo), z: 8, core: 2. Of those that a mesh axis runs over, the one named last changes fastest.
Arguments:
- inputs: bfloat16 [32768, 4096], P('ctx', 'head'), may hold values from -6 to 6
- queries: bfloat16 [32768, 2048], P('ctx', 'head'), may hold values from -25 to 25
- key_rows: bfloat16 [32768, 2048], P('ctx', 'head'), may hold values from -7 to 7
- value_rows: bfloat16 [32768, 2048], P('ctx', 'head'), may hold values from -6 to 6
- output_gradient: bfloat16 [32768, 4096], P('ctx', 'head'), may hold values from -6 to 6
- head_gradients: bfloat16 [32768, 2048], P('ctx', 'head'), may hold values from -6 to 6
- head_shift: int32 [16], P('head'), may hold values from 0 to 1, as said below
- down_qkv: bfloat16 [3, 4096, 16], P(None, 'head'), may hold values from -0.09375 to 0.09375
- up_qkv: bfloat16 [3, 16, 2048], P(None, None, 'head'), may hold values from -0.125 to 0.125
- output_down_adapter: bfloat16 [2048, 16], P('head'), may hold values from -0.125 to 0.125
- up_out: bfloat16 [16, 4096], P(None, 'head'), may hold values from -0.09375 to 0.09375
Outputs:
- projection_gradients: bfloat16 [3, 32768, 2048], P(None, 'ctx', 'head')
- projection_down_gradient: float32 [3, 4096, 16], P(None, 'head')
- projection_up_gradient: float32 [3, 16, 2048], P(None, None, 'head')
- output_down_gradient: float32 [2048, 16], P('head')
- output_up_gradient: float32 [16, 4096], P(None, 'head')
Inputs may be any that keep to these rules, and one draw needn't show every extreme that they name: `head_shift`: exactly half of the 16 heads are shifted.
All inputs are finite; a program needn't handle non-finite values.
Results may differ from a plain program's by a relative error of at most 0.015.
Values may be sent and summed in bfloat16 or wider, within the bound.
No kernel may reach another device: no remote copies, remote signals or barrier semaphores. Data moves between devices by JAX's collectives and lax.ppermute only.
A program may use at most 64 MiB of HBM per device.

v0:
```python
import jax
import jax.numpy as jnp
from jax import lax
from jax.sharding import PartitionSpec as P

GROUP = 2048


adapter_scale = 2.0


def as_sent(x):
    return jax.tree.map(lambda a: a.astype(jnp.bfloat16) if a.dtype == jnp.float32 else a, x)


def shifted(x, axis, by):
    count = lax.axis_size(axis)
    pairs = [(i, i + by) for i in range(count) if 0 <= i + by < count]
    return lax.ppermute(x, axis, pairs)


def shifted_2(x, axis, by):
    count = lax.axis_size(axis)
    return lax.ppermute(x, axis, [(i, (i + by) % count) for i in range(count)])


def attend(
    frame_query,
    frame_key,
    frame_value,
    frame_grad,
    position,
    shards_group,
    head_dim,
    fetch_keys,
    return_terms,
):
    rows_here, width = frame_query.shape
    heads_here = width // head_dim
    near_key = [frame_key]
    near_value = [frame_value]
    for offset in range(1, shards_group):
        moved_key, moved_value = fetch_keys((frame_key, frame_value), offset)
        near_key.append(moved_key)
        near_value.append(moved_value)
    keys_all = jnp.stack(near_key)
    values_all = jnp.stack(near_value)
    key_span = shards_group * rows_here
    column = lax.broadcasted_iota(jnp.int32, (rows_here, key_span), 1)
    row_index = lax.broadcasted_iota(jnp.int32, (rows_here, key_span), 0)
    key_block = column // rows_here
    inside = (key_block > 0) | (column % rows_here <= row_index)
    factor = head_dim ** (-0.5)
    query_grads, key_terms, value_terms, outputs = ([], [], [], [])
    for head_index in range(heads_here):
        start = head_index * head_dim
        query_head = frame_query[:, start : start + head_dim]
        grad_head = frame_grad[:, start : start + head_dim]
        key_head = keys_all[:, :, start : start + head_dim].reshape(key_span, head_dim)
        value_head = values_all[:, :, start : start + head_dim].reshape(key_span, head_dim)
        visible = inside & (key_block <= position[head_index])
        scores = (
            jnp.einsum("td,sd->ts", query_head, key_head, preferred_element_type=jnp.float32)
            * factor
        )
        scores = jnp.where(visible, scores, -1e30)
        row_peak = jnp.max(scores, axis=1, keepdims=True)
        weights = jnp.where(visible, jnp.exp(scores - row_peak), 0.0)
        attention = weights / jnp.sum(weights, axis=1, keepdims=True)
        attention_bf = attention.astype(jnp.bfloat16)
        out_head = jnp.dot(attention_bf, value_head, preferred_element_type=jnp.float32).astype(
            jnp.bfloat16
        )
        row_delta = jnp.sum(
            grad_head.astype(jnp.float32) * out_head.astype(jnp.float32), axis=1, keepdims=True
        )
        dprob = jnp.einsum("td,sd->ts", grad_head, value_head, preferred_element_type=jnp.float32)
        dscore = (attention * (dprob - row_delta)).astype(jnp.bfloat16)
        query_grads.append(
            (jnp.dot(dscore, key_head, preferred_element_type=jnp.float32) * factor).astype(
                jnp.bfloat16
            )
        )
        key_terms.append(
            jnp.einsum("ts,td->sd", dscore, query_head, preferred_element_type=jnp.float32) * factor
        )
        value_terms.append(
            jnp.einsum("ts,td->sd", attention_bf, grad_head, preferred_element_type=jnp.float32)
        )
        outputs.append(out_head)
    key_all = jnp.concatenate(key_terms, axis=1).reshape(shards_group, rows_here, width)
    value_all = jnp.concatenate(value_terms, axis=1).reshape(shards_group, rows_here, width)
    key_grad = key_all[0]
    value_grad = value_all[0]
    for offset in range(1, shards_group):
        back_key, back_value = return_terms(
            (key_all[offset].astype(jnp.bfloat16), value_all[offset].astype(jnp.bfloat16)), offset
        )
        key_grad = key_grad + back_key.astype(jnp.float32)
        value_grad = value_grad + back_value.astype(jnp.float32)
    grad_query = jnp.concatenate(query_grads, axis=1)
    attn_frame = jnp.concatenate(outputs, axis=1)
    return (grad_query, key_grad.astype(jnp.bfloat16), value_grad.astype(jnp.bfloat16), attn_frame)


def shards(
    inputs,
    queries,
    key_rows,
    value_rows,
    output_gradient,
    head_gradients,
    head_shift,
    down_qkv,
    up_qkv,
    output_down_adapter,
    up_out,
):
    rows_here, width = queries.shape
    heads_here = head_shift.shape[0]
    head_dim = width // heads_here
    shards_group = GROUP // rows_here
    half_shards = shards_group // 2
    place = lax.axis_index("ctx")
    input_part = jnp.einsum("td,kdr->ktr", inputs, down_qkv, preferred_element_type=jnp.float32)
    output_part = jnp.einsum(
        "td,rd->tr", output_gradient, up_out, preferred_element_type=jnp.float32
    )
    input_sum, output_sum = lax.psum((input_part, output_part), "head")
    input_lowrank = input_sum.astype(jnp.bfloat16)
    output_rank_product = output_sum.astype(jnp.bfloat16)
    attention_gradient = (
        head_gradients.astype(jnp.float32)
        + adapter_scale
        * jnp.einsum(
            "fq,zq->fz",
            output_rank_product,
            output_down_adapter,
            preferred_element_type=jnp.float32,
        )
    ).astype(jnp.bfloat16)
    col_shift = jnp.repeat(head_shift, head_dim) > 0

    def chain_fetch(pair, offset):
        return jax.tree.map(
            lambda part, own: part.astype(own.dtype), shifted(as_sent(pair), "ctx", offset), pair
        )

    def chain_return(pair, offset):
        return jax.tree.map(
            lambda part, own: part.astype(own.dtype), shifted(as_sent(pair), "ctx", -offset), pair
        )

    moved = shifted_2((queries, key_rows, value_rows, attention_gradient), "ctx", -half_shards)
    framed = [
        jnp.where(col_shift, moved_one, own)
        for moved_one, own in zip(moved, (queries, key_rows, value_rows, attention_gradient))
    ]
    position = jnp.zeros((heads_here,), jnp.int32) + place % shards_group
    results = attend(
        framed[0],
        framed[1],
        framed[2],
        framed[3],
        position,
        shards_group,
        head_dim,
        chain_fetch,
        chain_return,
    )
    returned = shifted_2((results[0], results[1], results[2], results[3]), "ctx", half_shards)
    grad_query, grad_key, grad_value, attention_result = [
        jnp.where(col_shift, back_one, own) for back_one, own in zip(returned, results)
    ]
    projection_gradients = jnp.stack([grad_query, grad_key, grad_value])
    grad_part = jnp.einsum(
        "ktc,krc->ktr", projection_gradients, up_qkv, preferred_element_type=jnp.float32
    )
    out_part = jnp.einsum(
        "tc,cr->tr", attention_result, output_down_adapter, preferred_element_type=jnp.float32
    )
    grad_sum, out_sum = lax.psum((grad_part, out_part), "head")
    rank_gradient = grad_sum.astype(jnp.bfloat16)
    output_lowrank = out_sum.astype(jnp.bfloat16)
    resident_projection_down = adapter_scale * jnp.einsum(
        "nj,gnb->gjb", inputs, rank_gradient, preferred_element_type=jnp.float32
    )
    resident_projection_up = adapter_scale * jnp.einsum(
        "diy,dio->dyo", input_lowrank, projection_gradients, preferred_element_type=jnp.float32
    )
    resident_output_down = adapter_scale * jnp.einsum(
        "pu,pq->uq", attention_result, output_rank_product, preferred_element_type=jnp.float32
    )
    resident_output_up = adapter_scale * jnp.einsum(
        "qw,qj->wj", output_lowrank, output_gradient, preferred_element_type=jnp.float32
    )
    summed = lax.psum(
        (
            resident_projection_down,
            resident_projection_up,
            resident_output_down,
            resident_output_up,
        ),
        "ctx",
    )
    norm_value = (rows_here * lax.axis_size("ctx")) ** (-0.5)
    return (
        projection_gradients,
        summed[0] * norm_value,
        summed[1] * norm_value,
        summed[2] * norm_value,
        summed[3] * norm_value,
    )


def solution(mesh):
    placed = (
        P("ctx", "head"),
        P("ctx", "head"),
        P("ctx", "head"),
        P("ctx", "head"),
        P("ctx", "head"),
        P("ctx", "head"),
        P("head"),
        P(None, "head", None),
        P(None, None, "head"),
        P("head", None),
        P(None, "head"),
    )
    return jax.shard_map(
        shards,
        mesh=mesh,
        in_specs=placed,
        out_specs=(
            P(None, "ctx", "head"),
            P(None, "head", None),
            P(None, None, "head"),
            P("head", None),
            P(None, "head"),
        ),
        check_vma=False,
    )
```

profile of v0, /device:TPU:8, one launch (start us, length us, event | category | flops | bytes accessed | tf_op | source)
XLA Modules:
  0.0 1166.7 jit_solution(2827487544569865493)
XLA Ops:
  7.2 1.7 fusion.79
  9.0 10.3 psum.56
  19.2 1.3 copy.30
  20.5 1.1 fusion.15
  21.6 10.7 collective-permute-start.5
  32.3 1.3 copy.31
  33.5 1.5 collective-permute-start.6
  35.4 1.3 copy.25
  36.8 47.2 %collective-permute-done.5 = bf16[512,512]{0,1:T(8,128)(2,1)} collective-permute-done((bf16[512,512]{0,1:T(8,128)(2,1)S(1)}, bf16[512,512]{0,1:T(8,128)(2,1)}, u32[]{:S(2)}, u32[]{:S(2)}) %collective-permute-start.5) | collective-permute-done | bytes 524320 | tf_op jit(solution)/shard_map/ppermute | solution.py:24
  84.1 11.2 collective-permute-done.6
  95.3 11.2 collective-permute-done.1
  106.5 15.4 %collective-permute-done = bf16[512,512]{0,1:T(8,128)(2,1)S(1)} collective-permute-done((bf16[512,512]{0,1:T(8,128)(2,1)S(1)}, bf16[512,512]{0,1:T(8,128)(2,1)S(1)}, u32[]{:S(2)}, u32[]{:S(2)}) %collective-permute-start) | collective-permute-done | bytes 524320 | tf_op jit(solution)/shard_map/ppermute | solution.py:24
  122.0 3.0 broadcast_select_fusion.1
  125.0 1.3 collective-permute-start.9
  126.3 1.3 collective-permute-start.8
  127.6 9.2 collective-permute-start.7
  136.8 2.7 collective-permute-start.4
  139.5 3.1 collective-permute-start.3
  142.6 19.8 %collective-permute-done.9 = bf16[512,512]{0,1:T(8,128)(2,1)S(1)} collective-permute-done((bf16[512,512]{0,1:T(8,128)(2,1)}, bf16[512,512]{0,1:T(8,128)(2,1)S(1)}, u32[]{:S(2)}, u32[]{:S(2)}) %collective-permute-start.9) | collective-permute-done | bytes 524320 | tf_op jit(solution)/shard_map/ppermute | solution.py:19
  162.4 2.2 collective-permute-start.2
  164.7 9.6 collective-permute-done.8
  174.3 21.0 %collective-permute-done.7 = bf16[512,512]{0,1:T(8,128)(2,1)S(1)} collective-permute-done((bf16[512,512]{0,1:T(8,128)(2,1)}, bf16[512,512]{0,1:T(8,128)(2,1)S(1)}, u32[]{:S(2)}, u32[]{:S(2)}) %collective-permute-start.7) | collective-permute-done | bytes 524320 | tf_op jit(solution)/shard_map/ppermute | solution.py:19
  195.4 1.3 pad_maximum_fusion.3
  196.7 1.0 fusion.76
  197.7 2.1 copy.37
  199.7 1.0 copy.39
  200.8 1.0 copy.35
  202.8 27.1 %collective-permute-done.4 = bf16[512,512]{0,1:T(8,128)(2,1)} collective-permute-done((bf16[512,512]{0,1:T(8,128)(2,1)}, bf16[512,512]{0,1:T(8,128)(2,1)}, u32[]{:S(2)}, u32[]{:S(2)}) %collective-permute-start.4) | collective-permute-done | bytes 524320 | tf_op jit(solution)/shard_map/ppermute | solution.py:19
  229.9 11.9 %collective-permute-done.3 = bf16[512,512]{0,1:T(8,128)(2,1)} collective-permute-done((bf16[512,512]{0,1:T(8,128)(2,1)}, bf16[512,512]{0,1:T(8,128)(2,1)}, u32[]{:S(2)}, u32[]{:S(2)}) %collective-permute-start.3) | collective-permute-done | bytes 524320 | tf_op jit(solution)/shard_map/ppermute | solution.py:19
  241.9 19.9 %collective-permute-done.2 = bf16[512,512]{0,1:T(8,128)(2,1)} collective-permute-done((bf16[512,512]{0,1:T(8,128)(2,1)}, bf16[512,512]{0,1:T(8,128)(2,1)}, u32[]{:S(2)}, u32[]{:S(2)}) %collective-permute-start.2) | collective-permute-done | bytes 524320 | tf_op jit(solution)/shard_map/ppermute | solution.py:19
  261.7 1.8 pad_maximum_fusion.2
  263.5 1.2 fusion.78
  264.9 1.5 copy.38
  266.5 1.0 copy.34
  267.5 1.3 copy.29
  270.3 1.3 fusion.2
  271.7 4.9 fusion.7
  276.6 5.8 fusion.9
  282.4 4.5 fusion.8
  286.9 1.9 convolution_convert_fusion.2
  302.7 1.4 collective-permute-start.11
  304.1 1.3 collective-permute-start.13
  305.4 1.3 collective-permute-start.12
  306.9 1.3 collective-permute-start.15
  308.2 1.5 collective-permute-start.17
  311.4 9.6 collective-permute-done.11
  321.0 1.3 collective-permute-start.16
  322.4 43.4 %collective-permute-done.13 = bf16[512,512]{0,1:T(8,128)(2,1)S(1)} collective-permute-done((bf16[512,512]{0,1:T(8,128)(2,1)S(1)}, bf16[512,512]{0,1:T(8,128)(2,1)S(1)}, u32[]{:S(2)}, u32[]{:S(2)}) %collective-permute-start.13) | collective-permute-done | bytes 524320 | tf_op jit(solution)/shard_map/ppermute | solution.py:19
  365.8 5.1 collective-permute-start.19
  371.1 31.7 %collective-permute-start.14 = (bf16[512,512]{0,1:T(8,128)(2,1)S(1)}, bf16[512,512]{0,1:T(8,128)(2,1)S(1)}, u32[]{:S(2)}, u32[]{:S(2)}) collective-permute-start(bf16[512,512]{0,1:T(8,128)(2,1)S(1)} %fusion.26), channel_id=1, source_target_pairs={{0,8},{4,12},{8,16},{12,20},{16,24},{20,28},{24,32},{28,36},{32,40... | collective-permute-start | bytes 1572872 | tf_op jit(solution)/shard_map/ppermute | solution.py:24
  402.8 30.4 %collective-permute-done.17 = bf16[512,512]{0,1:T(8,128)(2,1)S(1)} collective-permute-done((bf16[512,512]{0,1:T(8,128)(2,1)S(1)}, bf16[512,512]{0,1:T(8,128)(2,1)S(1)}, u32[]{:S(2)}, u32[]{:S(2)}) %collective-permute-start.17) | collective-permute-done | bytes 524320 | tf_op jit(solution)/shard_map/ppermute | solution.py:19
  433.5 3.2 collective-permute-start.18
  437.2 1.2 fusion.72
  438.4 16.7 %collective-permute-done.18 = bf16[512,512]{0,1:T(8,128)(2,1)S(1)} collective-permute-done((bf16[512,512]{0,1:T(8,128)(2,1)S(1)}, bf16[512,512]{0,1:T(8,128)(2,1)S(1)}, u32[]{:S(2)}, u32[]{:S(2)}) %collective-permute-start.18) | collective-permute-done | bytes 524320 | tf_op jit(solution)/shard_map/ppermute | solution.py:24
  456.0 21.2 %all-reduce.6 = (bf16[3,512,16]{1,2,0:T(8,128)(2,1)S(1)}, bf16[3,512,16]{1,2,0:T(8,128)(2,1)}, bf16[512,16]{1,0:T(8,128)(2,1)S(1)}) all-reduce(f32[3,512,16]{1,2,0:T(8,128)S(1)} %fusion.80, f32[3,512,16]{1,2,0:T(8,128)S(1)} %convolution_bitcast_fusion, f32[512,16]{1,0:T(8,128)} %fusion.72), channel_id=1, replica_groups=mesh['ctx'=64,'head'=4] {'head'}, use_global_device_ids=true, to_apply=%region_13.14 | all-reduce | flops 57344 | bytes 344064 | tf_op jit(solution)/shard_map/psum | solution.py:182
  477.3 2.1 convolution_multiply_fusion.11
  479.4 2.0 convolution_multiply_fusion.10
  482.4 1.4 convolution_multiply_fusion.12
  483.8 361.9 %psum.61 = f32[512,16]{0,1:T(8,128)S(1)} all-reduce(f32[512,16]{0,1:T(8,128)S(1)} %convolution_multiply_fusion.12), channel_id=1, replica_groups=mesh['ctx'=64,'head'=4] {'ctx'}, use_global_device_ids=true, to_apply=%region_17.18 | all-reduce | flops 8192 | bytes 65536 | tf_op jit(solution)/shard_map/psum | solution.py:197
  846.3 1.6 copy.41
  847.9 306.9 %all-reduce.5.cloned.1.call-done = (f32[3,1024,16]{1,2,0:T(8,128)}, f32[3,16,512]{2,1,0:T(8,128)}, f32[16,1024]{1,0:T(8,128)}) async-done(((f32[3,1024,16]{1,2,0:T(8,128)}, f32[3,16,512]{2,1,0:T(8,128)}, f32[16,1024]{1,0:T(8,128)}), (f32[3,1024,16]{1,2,0:T(8,128)}, f32[3,16,512]{2,1,0:T(8,128)}, f32[16,1024]{1,0:T(8,128)})) %all-reduce.5.cloned.1.call-update) | async-done | bytes 360464 | tf_op jit(solution)/shard_map/psum | solution.py:197
  1154.8 1.6 broadcast_multiply_fusion
  1156.4 1.5 broadcast_multiply_fusion.2
  1157.9 1.5 broadcast_multiply_fusion.1
  (106 shorter events, 22.3 us)
Async XLA Ops:
  7.2 429.5 %copy-start = (bf16[512,1024]{1,0:T(8,128)(2,1)S(1)}, bf16[512,1024]{1,0:T(8,128)(2,1)}, u32[]{:S(2)}) copy-start(bf16[512,1024]{1,0:T(8,128)(2,1)} %param.11) | copy-start | bytes 3145732
  7.2 27.9 %copy-start.17 = (bf16[512,512]{1,0:T(8,128)(2,1)S(1)}, bf16[512,512]{1,0:T(8,128)(2,1)}, u32[]{:S(2)}) copy-start(bf16[512,512]{1,0:T(8,128)(2,1)} %param.13) | copy-start | bytes 1572868
  7.2 29.6 %copy-start.24 = (s32[4]{0:T(128)S(1)}, s32[4]{0:T(128)}, u32[]{:S(2)}) copy-start(s32[4]{0:T(128)} %param.17) | copy-start | bytes 52
  7.2 1147.6 %all-reduce.5.cloned.1.call-start = ((), (), s32[]{:S(2)}) async-start(), calls=%async_computation | async-start | bytes 720896 | tf_op jit(solution)/shard_map/psum | solution.py:197
  21.6 62.5 %collective-permute-start.5 = (bf16[512,512]{0,1:T(8,128)(2,1)S(1)}, bf16[512,512]{0,1:T(8,128)(2,1)}, u32[]{:S(2)}, u32[]{:S(2)}) collective-permute-start(bf16[512,512]{0,1:T(8,128)(2,1)S(1)} %fusion.15), channel_id=1, source_target_pairs={{0,248},{4,252},{8,0},{12,4},{16,8},{20,12},{24,16},{28,20},{32,24... | collective-permute-start | bytes 1572872 | tf_op jit(solution)/shard_map/ppermute | solution.py:24
  33.5 61.8 %collective-permute-start.6 = (bf16[512,512]{0,1:T(8,128)(2,1)S(1)}, bf16[512,512]{0,1:T(8,128)(2,1)}, u32[]{:S(2)}, u32[]{:S(2)}) collective-permute-start(bf16[512,512]{0,1:T(8,128)(2,1)S(1)} %copy.31), channel_id=1, source_target_pairs={{0,248},{4,252},{8,0},{12,4},{16,8},{20,12},{24,16},{28,20},{32,24... | collective-permute-start | bytes 1572872 | tf_op jit(solution)/shard_map/ppermute | solution.py:24
  35.3 71.3 %collective-permute-start.1 = (bf16[512,512]{0,1:T(8,128)(2,1)S(1)}, bf16[512,512]{0,1:T(8,128)(2,1)}, u32[]{:S(2)}, u32[]{:S(2)}) collective-permute-start(bf16[512,512]{0,1:T(8,128)(2,1)S(1)} %copy.27), channel_id=1, source_target_pairs={{0,248},{4,252},{8,0},{12,4},{16,8},{20,12},{24,16},{28,20},{32,24... | collective-permute-start | bytes 1572872 | tf_op jit(solution)/shard_map/ppermute | solution.py:24
  36.6 69.9 %copy-start.12 = (bf16[512,512]{0,1:T(8,128)(2,1)}, bf16[512,512]{0,1:T(8,128)(2,1)S(1)}, u32[]{:S(2)}) copy-start(bf16[512,512]{0,1:T(8,128)(2,1)S(1)} %copy.25) | copy-start | bytes 1572868
  36.6 85.3 %collective-permute-start = (bf16[512,512]{0,1:T(8,128)(2,1)S(1)}, bf16[512,512]{0,1:T(8,128)(2,1)S(1)}, u32[]{:S(2)}, u32[]{:S(2)}) collective-permute-start(bf16[512,512]{0,1:T(8,128)(2,1)S(1)} %copy.25), channel_id=1, source_target_pairs={{0,248},{4,252},{8,0},{12,4},{16,8},{20,12},{24,16},{28,20},{32,24... | collective-permute-start | bytes 1572872 | tf_op jit(solution)/shard_map/ppermute | solution.py:24
  36.8 418.3 %copy-start.21 = (pred[512]{0:T(512)(128)(4,1)}, pred[512]{0:T(512)(128)(4,1)S(1)}, u32[]{:S(2)}) copy-start(pred[512]{0:T(512)(128)(4,1)S(1)} %broadcast_bitcast_fusion) | copy-start | bytes 1540
  125.0 145.3 %copy-start.10 = (bf16[512,512]{0,1:T(8,128)(2,1)}, bf16[512,512]{0,1:T(8,128)(2,1)S(1)}, u32[]{:S(2)}) copy-start(bf16[512,512]{0,1:T(8,128)(2,1)S(1)} %get-tuple-element.56) | copy-start | bytes 1572868
  125.0 37.5 %collective-permute-start.9 = (bf16[512,512]{0,1:T(8,128)(2,1)}, bf16[512,512]{0,1:T(8,128)(2,1)S(1)}, u32[]{:S(2)}, u32[]{:S(2)}) collective-permute-start(bf16[512,512]{0,1:T(8,128)(2,1)} %get-tuple-element.53), channel_id=1, source_target_pairs={{0,12},{4,16},{8,20},{12,24},{16,28},{20,32},{24,36},{28,40},{32,4... | collective-permute-start | bytes 1572872 | tf_op jit(solution)/shard_map/ppermute | solution.py:19
  126.3 48.0 %collective-permute-start.8 = (bf16[512,512]{0,1:T(8,128)(2,1)}, bf16[512,512]{0,1:T(8,128)(2,1)S(1)}, u32[]{:S(2)}, u32[]{:S(2)}) collective-permute-start(bf16[512,512]{0,1:T(8,128)(2,1)} %get-tuple-element.53), channel_id=1, source_target_pairs={{0,8},{4,12},{8,16},{12,20},{16,24},{20,28},{24,32},{28,36},{32,40... | collective-permute-start | bytes 1572872 | tf_op jit(solution)/shard_map/ppermute | solution.py:19
  127.6 67.7 %collective-permute-start.7 = (bf16[512,512]{0,1:T(8,128)(2,1)}, bf16[512,512]{0,1:T(8,128)(2,1)S(1)}, u32[]{:S(2)}, u32[]{:S(2)}) collective-permute-start(bf16[512,512]{0,1:T(8,128)(2,1)} %get-tuple-element.53), channel_id=1, source_target_pairs={{0,4},{4,8},{8,12},{12,16},{16,20},{20,24},{24,28},{28,32},{32,36}... | collective-permute-start | bytes 1572872 | tf_op jit(solution)/shard_map/ppermute | solution.py:19
  136.8 93.1 %collective-permute-start.4 = (bf16[512,512]{0,1:T(8,128)(2,1)}, bf16[512,512]{0,1:T(8,128)(2,1)}, u32[]{:S(2)}, u32[]{:S(2)}) collective-permute-start(bf16[512,512]{0,1:T(8,128)(2,1)} %get-tuple-element.54), channel_id=1, source_target_pairs={{0,12},{4,16},{8,20},{12,24},{16,28},{20,32},{24,36},{28,40},{32,4... | collective-permute-start | bytes 1572872 | tf_op jit(solution)/shard_map/ppermute | solution.py:19
  139.5 102.3 %collective-permute-start.3 = (bf16[512,512]{0,1:T(8,128)(2,1)}, bf16[512,512]{0,1:T(8,128)(2,1)}, u32[]{:S(2)}, u32[]{:S(2)}) collective-permute-start(bf16[512,512]{0,1:T(8,128)(2,1)} %get-tuple-element.54), channel_id=1, source_target_pairs={{0,8},{4,12},{8,16},{12,20},{16,24},{20,28},{24,32},{28,36},{32,40... | collective-permute-start | bytes 1572872 | tf_op jit(solution)/shard_map/ppermute | solution.py:19
  162.4 99.3 %collective-permute-start.2 = (bf16[512,512]{0,1:T(8,128)(2,1)}, bf16[512,512]{0,1:T(8,128)(2,1)}, u32[]{:S(2)}, u32[]{:S(2)}) collective-permute-start(bf16[512,512]{0,1:T(8,128)(2,1)} %get-tuple-element.54), channel_id=1, source_target_pairs={{0,4},{4,8},{8,12},{12,16},{16,20},{20,24},{24,28},{28,32},{32,36}... | collective-permute-start | bytes 1572872 | tf_op jit(solution)/shard_map/ppermute | solution.py:19
  264.9 5.3 copy-start.7
  266.5 3.8 copy-start.5
  268.8 1.5 copy-start.13
  270.3 1.4 copy-start.15
  286.9 2.0 copy-start.1
  286.9 2.5 copy-start.3
  288.9 1.4 copy-start.2
  289.4 1.7 copy-start.9
  290.3 1.8 copy-start.4
  292.1 1.0 copy-start.16
  292.1 1.9 copy-start.11
  294.9 1.0 copy-start.8
  302.5 7.2 copy-start.6
  302.5 8.0 copy-start.14
  302.7 18.3 %collective-permute-start.11 = (bf16[512,512]{0,1:T(8,128)(2,1)S(1)}, bf16[512,512]{0,1:T(8,128)(2,1)S(1)}, u32[]{:S(2)}, u32[]{:S(2)}) collective-permute-start(bf16[512,512]{0,1:T(8,128)(2,1)S(1)} %get-tuple-element.32), channel_id=1, source_target_pairs={{4,0},{8,4},{12,8},{16,12},{20,16},{24,20},{28,24},{32,28},{36,32}... | collective-permute-start | bytes 1572872 | tf_op jit(solution)/shard_map/ppermute | solution.py:19
  304.1 61.6 %collective-permute-start.13 = (bf16[512,512]{0,1:T(8,128)(2,1)S(1)}, bf16[512,512]{0,1:T(8,128)(2,1)S(1)}, u32[]{:S(2)}, u32[]{:S(2)}) collective-permute-start(bf16[512,512]{0,1:T(8,128)(2,1)S(1)} %get-tuple-element.33), channel_id=1, source_target_pairs={{12,0},{16,4},{20,8},{24,12},{28,16},{32,20},{36,24},{40,28},{44,3... | collective-permute-start | bytes 1572872 | tf_op jit(solution)/shard_map/ppermute | solution.py:19
  305.4 65.4 %collective-permute-start.12 = (bf16[512,512]{0,1:T(8,128)(2,1)S(1)}, bf16[512,512]{0,1:T(8,128)(2,1)S(1)}, u32[]{:S(2)}, u32[]{:S(2)}) collective-permute-start(bf16[512,512]{0,1:T(8,128)(2,1)S(1)} %get-tuple-element.34), channel_id=1, source_target_pairs={{8,0},{12,4},{16,8},{20,12},{24,16},{28,20},{32,24},{36,28},{40,32... | collective-permute-start | bytes 1572872 | tf_op jit(solution)/shard_map/ppermute | solution.py:19
  306.9 64.3 %collective-permute-start.15 = (bf16[512,512]{0,1:T(8,128)(2,1)S(1)}, bf16[512,512]{0,1:T(8,128)(2,1)S(1)}, u32[]{:S(2)}, u32[]{:S(2)}) collective-permute-start(bf16[512,512]{0,1:T(8,128)(2,1)S(1)} %get-tuple-element.39), channel_id=1, source_target_pairs={{4,0},{8,4},{12,8},{16,12},{20,16},{24,20},{28,24},{32,28},{36,32}... | collective-permute-start | bytes 1572872 | tf_op jit(solution)/shard_map/ppermute | solution.py:19
  308.2 125.1 %collective-permute-start.17 = (bf16[512,512]{0,1:T(8,128)(2,1)S(1)}, bf16[512,512]{0,1:T(8,128)(2,1)S(1)}, u32[]{:S(2)}, u32[]{:S(2)}) collective-permute-start(bf16[512,512]{0,1:T(8,128)(2,1)S(1)} %get-tuple-element.40), channel_id=1, source_target_pairs={{12,0},{16,4},{20,8},{24,12},{28,16},{32,20},{36,24},{40,28},{44,3... | collective-permute-start | bytes 1572872 | tf_op jit(solution)/shard_map/ppermute | solution.py:19
  321.0 112.3 %collective-permute-start.16 = (bf16[512,512]{0,1:T(8,128)(2,1)S(1)}, bf16[512,512]{0,1:T(8,128)(2,1)S(1)}, u32[]{:S(2)}, u32[]{:S(2)}) collective-permute-start(bf16[512,512]{0,1:T(8,128)(2,1)S(1)} %get-tuple-element.41), channel_id=1, source_target_pairs={{8,0},{12,4},{16,8},{20,12},{24,16},{28,20},{32,24},{36,28},{40,32... | collective-permute-start | bytes 1572872 | tf_op jit(solution)/shard_map/ppermute | solution.py:19
  322.2 114.5 %copy-start.18 = (bf16[3,1024,16]{1,2,0:T(8,128)(2,1)S(1)}, bf16[3,1024,16]{1,2,0:T(8,128)(2,1)}, u32[]{:S(2)}) copy-start(bf16[3,1024,16]{1,2,0:T(8,128)(2,1)} %param.18) | copy-start | bytes 294916
  322.3 114.9 %copy-start.20 = (bf16[512,16]{0,1:T(8,128)(2,1)S(1)}, bf16[512,16]{0,1:T(8,128)(2,1)}, u32[]{:S(2)}) copy-start(bf16[512,16]{0,1:T(8,128)(2,1)} %param.20) | copy-start | bytes 49156
  365.8 71.4 %collective-permute-start.19 = (bf16[512,512]{0,1:T(8,128)(2,1)S(1)}, bf16[512,512]{0,1:T(8,128)(2,1)S(1)}, u32[]{:S(2)}, u32[]{:S(2)}) collective-permute-start(bf16[512,512]{0,1:T(8,128)(2,1)S(1)} %pad_maximum_fusion.6), channel_id=1, source_target_pairs={{0,8},{4,12},{8,16},{12,20},{16,24},{20,28},{24,32},{28,36},{32,40... | collective-permute-start | bytes 1572872 | tf_op jit(solution)/shard_map/ppermute | solution.py:24
  370.8 67.5 %collective-permute-start.10 = (bf16[512,512]{0,1:T(8,128)(2,1)S(1)}, bf16[512,512]{0,1:T(8,128)(2,1)S(1)}, u32[]{:S(2)}, u32[]{:S(2)}) collective-permute-start(bf16[512,512]{0,1:T(8,128)(2,1)S(1)} %pad_maximum_fusion.5), channel_id=1, source_target_pairs={{0,8},{4,12},{8,16},{12,20},{16,24},{20,28},{24,32},{28,36},{32,40... | collective-permute-start | bytes 1572872 | tf_op jit(solution)/shard_map/ppermute | solution.py:24
  371.1 67.2 %collective-permute-start.14 = (bf16[512,512]{0,1:T(8,128)(2,1)S(1)}, bf16[512,512]{0,1:T(8,128)(2,1)S(1)}, u32[]{:S(2)}, u32[]{:S(2)}) collective-permute-start(bf16[512,512]{0,1:T(8,128)(2,1)S(1)} %fusion.26), channel_id=1, source_target_pairs={{0,8},{4,12},{8,16},{12,20},{16,24},{20,28},{24,32},{28,36},{32,40... | collective-permute-start | bytes 1572872 | tf_op jit(solution)/shard_map/ppermute | solution.py:24
  433.5 21.6 %collective-permute-start.18 = (bf16[512,512]{0,1:T(8,128)(2,1)S(1)}, bf16[512,512]{0,1:T(8,128)(2,1)S(1)}, u32[]{:S(2)}, u32[]{:S(2)}) collective-permute-start(bf16[512,512]{0,1:T(8,128)(2,1)S(1)} %fusion.23), channel_id=1, source_target_pairs={{0,8},{4,12},{8,16},{12,20},{16,24},{20,28},{24,32},{28,36},{32,40... | collective-permute-start | bytes 1572872 | tf_op jit(solution)/shard_map/ppermute | solution.py:24
  437.2 18.6 %copy-start.23 = (bf16[512,512]{0,1:T(8,128)(2,1)}, bf16[512,512]{0,1:T(8,128)(2,1)S(1)}, u32[]{:S(2)}) copy-start(bf16[512,512]{0,1:T(8,128)(2,1)S(1)} %collective-permute-done.19) | copy-start | bytes 1572868
  438.3 17.4 %copy-start.19 = (bf16[3,16,512]{2,1,0:T(8,128)(2,1)S(1)}, bf16[3,16,512]{2,1,0:T(8,128)(2,1)}, u32[]{:S(2)}) copy-start(bf16[3,16,512]{2,1,0:T(8,128)(2,1)} %param.19) | copy-start | bytes 147460
  455.5 26.8 %copy-start.22 = (pred[512]{0:T(512)(128)(4,1)S(1)}, pred[512]{0:T(512)(128)(4,1)}, u32[]{:S(2)}) copy-start(pred[512]{0:T(512)(128)(4,1)} %copy-done.21) | copy-start | bytes 1540
Sparse Core Ops, SparseCore 0:
  482.5 672.2 all-reduce.4
where the time goes:
time: 1170 us
  waiting for transfers between devices  602 us (51%)
  blocking collectives  393 us (34%)
  starting transfers between devices  80.4 us (7%)
  matrix products  33.8 us (3%)
  other arithmetic  24.5 us (2%)
  local copies, waits for them, and re-layouts  17.7 us (2%)
  between operations  15.2 us (1%)
    psum x1, blocking collectives, shards(): lax.psum((resident_projection_down, resident_projection_up, resident_outp...  362 us
    psum x1, waiting for transfers between devices, shards(): lax.psum((resident_projection_down, resident_projection_up, resident_outp...  307 us
    ppermute x12, waiting for transfers between devices, shifted(): return lax.ppermute(x, axis, pairs)  193 us
    ppermute x8, waiting for transfers between devices, shifted_2(): return lax.ppermute(x, axis, [(i, (i + by) % count) for i in range(count)])  102 us
    ppermute x8, starting transfers between devices, shifted_2(): return lax.ppermute(x, axis, [(i, (i + by) % count) for i in range(count)])  52.4 us
    ppermute x12, starting transfers between devices, shifted(): return lax.ppermute(x, axis, pairs)  28 us
  transfers between devices with their start and end apart: 21, of which 15 were waited for; matrix products, arithmetic and copies ran while one was open for 2% of the time, Pallas kernels for 0%

commit v1 on v0

v1 whole, which is shorter than its diff:
```python
import functools

import jax
import jax.numpy as jnp
from jax import lax
from jax.experimental import pallas as pl
from jax.experimental.pallas import tpu as pltpu
from jax.sharding import PartitionSpec as P

adapter_scale = 2.0
F32 = jnp.float32
BF16 = jnp.bfloat16
ANY = pl.BlockSpec(memory_space=pl.ANY)
SMEM = pl.BlockSpec(memory_space=pltpu.SMEM)
VMEM = pl.BlockSpec(memory_space=pltpu.VMEM)

ROLE_OF_SLOT = ((3, 0, 2, 1), (0, 1, 3, 2), (1, 2, 0, 3), (2, 3, 1, 0))
SLOT_OF_ROLE = tuple(tuple(row.index(r) for r in range(4)) for row in ROLE_OF_SLOT)


def pick(index, values):
    out = jnp.int32(values[-1]) if isinstance(values[-1], int) else values[-1]
    for i in range(len(values) - 2, -1, -1):
        out = jnp.where(index == i, values[i], out)
    return out


def plan_kernel(shift_ref, me_ref, out_ref):
    place, column = me_ref[0], me_ref[1]
    quarter = lax.rem(place, 4)
    high, core = lax.div(column, 2), lax.rem(column, 2)
    shift = [shift_ref[i] for i in range(16)]
    excess = sum(shift[:8]) - 4
    swaps = jnp.abs(excess)
    low_swaps = lax.div(swaps, 2)
    core_swaps = (low_swaps, swaps - low_swaps)
    first_sends = jnp.where(excess > 0, 1, 0)
    sent_type = jnp.where(high == 0, first_sends, 1 - first_sends)
    other_type = 1 - sent_type
    mine = [jnp.where(high == 0, shift[i], shift[8 + i]) for i in range(8)]
    theirs = [jnp.where(high == 0, shift[8 + i], shift[i]) for i in range(8)]
    rank_sent = jnp.int32(0)
    rank_other = jnp.int32(0)
    kept, worker, role, column_rank = [], [], [], []
    for h in range(8):
        if h % 4 == 0:
            in_column = jnp.int32(0)
        is_sent = mine[h] == sent_type
        keep = jnp.logical_not(is_sent & (in_column < core_swaps[h // 4]))
        column_rank.append(in_column)
        at = jnp.where(is_sent, rank_sent, rank_other)
        room = 2 - core_swaps[0]
        on_core = jnp.where(is_sent, lax.div(at, 2), jnp.where(at < room, 0, 1))
        turn = jnp.where(is_sent, lax.rem(at, 2), jnp.where(at < room, at, at - room))
        kept.append(keep)
        worker.append(on_core)
        role.append(mine[h] * 2 + turn)
        in_column = in_column + jnp.where(is_sent, 1, 0)
        rank_sent = rank_sent + jnp.where(is_sent & keep, 1, 0)
        rank_other = rank_other + jnp.where(is_sent, 0, 1)
    source = [jnp.int32(9), jnp.int32(8), jnp.int32(9), jnp.int32(8)]
    for h in range(8):
        here = jnp.where(core == h // 4, h % 4, 4 + h % 4)
        for r in range(4):
            hit = kept[h] & (worker[h] == core) & (role[h] == r)
            source[r] = jnp.where(hit, here, source[r])
    slots = [pick(quarter, [ROLE_OF_SLOT[j][s] for j in range(4)]) for s in range(4)]
    for s in range(4):
        out_ref[s] = pick(slots[s], source)
    slot_of = [pick(quarter, [SLOT_OF_ROLE[j][r] for j in range(4)]) for r in range(4)]
    for want in range(2):
        out_index = jnp.int32(0)
        in_index = jnp.int32(0)
        seen = jnp.int32(0)
        for i in range(4):
            own = jnp.where(core == 0, mine[i], mine[4 + i])
            rank = jnp.where(core == 0, column_rank[i], column_rank[4 + i])
            out_index = jnp.where((own == sent_type) & (rank == want), i, out_index)
            far = jnp.where(core == 0, theirs[i], theirs[4 + i])
            in_index = jnp.where((far == other_type) & (seen == want), i, in_index)
            seen = seen + jnp.where(far == other_type, 1, 0)
        out_ref[4 + want] = out_index
        out_ref[14 + want] = in_index
    out_ref[6] = pick(other_type * 2 + 1, slot_of)
    out_ref[7] = pick(other_type * 2, slot_of)
    for i in range(4):
        keep = jnp.where(core == 0, kept[i], kept[4 + i])
        on_core = jnp.where(core == 0, worker[i], worker[4 + i])
        rank = jnp.where(core == 0, column_rank[i], column_rank[4 + i])
        which = jnp.where(core == 0, role[i], role[4 + i])
        back = pick(which, slot_of) + jnp.where(on_core == core, 0, 4)
        out_ref[8 + i] = jnp.where(keep, back, 8 + rank)
    out_ref[12] = jnp.minimum(swaps, 3)
    found = pick(slots[0], source)
    near = lax.rem(found, 4)
    out_ref[13] = jnp.where(
        found < 4,
        column * 4 + near,
        jnp.where(
            found < 8,
            (column + 1 - 2 * core) * 4 + near,
            (column + 2 - 4 * high) * 4 + jnp.where(found == 8, out_ref[14], out_ref[15]),
        ),
    )


def make_plan(shift_all, place, column):
    return pl.pallas_call(
        plan_kernel,
        out_shape=jax.ShapeDtypeStruct((16,), jnp.int32),
        in_specs=[SMEM, SMEM],
        out_specs=SMEM,
        name="plan",
    )(shift_all, jnp.stack([place, column]).astype(jnp.int32))


def column_of(ref, index, width):
    return ref.at[:, pl.ds(pl.multiple_of(index * width, width), width)]


def far_pack(plan, arrays, width):
    count = len(arrays)
    rows = arrays[0].shape[0]

    def body(plan_ref, *refs):
        own, out, sems = refs[:count], refs[count], refs[count + 1]
        copies = []
        for r in range(2):
            for t in range(count):
                copy = pltpu.make_async_copy(
                    column_of(own[t], plan_ref[4 + r], width), out.at[r, t], sems.at[r, t]
                )
                copy.start()
                copies.append(copy)
        for copy in copies:
            copy.wait()

    return pl.pallas_call(
        body,
        out_shape=jax.ShapeDtypeStruct((2, count, rows, width), arrays[0].dtype),
        in_specs=[SMEM] + [ANY] * count,
        out_specs=ANY,
        scratch_shapes=[pltpu.SemaphoreType.DMA((2, count))],
        name="far_pack",
    )(plan, *arrays)


def slot_pack(plan, own_arrays, sibling_arrays, far, width):
    count = len(own_arrays)
    rows = own_arrays[0].shape[0]

    def body(plan_ref, *refs):
        own, sib = refs[:count], refs[count : 2 * count]
        far_ref = refs[2 * count]
        outs = refs[2 * count + 1 : 2 * count + 5]
        sems = refs[2 * count + 5]
        for s in range(4):
            source = plan_ref[s]

            @pl.when(source < 4)
            def _(s=s, source=source):
                for t in range(count):
                    pltpu.make_async_copy(
                        column_of(own[t], source, width), outs[s].at[t], sems.at[s, t]
                    ).start()

            @pl.when((source >= 4) & (source < 8))
            def _(s=s, source=source):
                for t in range(count):
                    pltpu.make_async_copy(
                        column_of(sib[t], source - 4, width), outs[s].at[t], sems.at[s, t]
                    ).start()

            @pl.when(source >= 8)
            def _(s=s, source=source):
                for t in range(count):
                    pltpu.make_async_copy(
                        far_ref.at[source - 8, t], outs[s].at[t], sems.at[s, t]
                    ).start()

        for s in range(4):
            for t in range(count):
                pltpu.make_async_copy(far_ref.at[0, t], outs[s].at[t], sems.at[s, t]).wait()

    return pl.pallas_call(
        body,
        out_shape=[jax.ShapeDtypeStruct((count, rows, width), own_arrays[0].dtype)] * 4,
        in_specs=[SMEM] + [ANY] * (2 * count + 1),
        out_specs=[ANY] * 4,
        scratch_shapes=[pltpu.SemaphoreType.DMA((4, count))],
        name="slot_pack",
    )(plan, *own_arrays, *sibling_arrays, far)


def far_return_pack(plan, slots):
    count, rows, width = slots[0].shape

    def body(plan_ref, *refs):
        ins, out, sems = refs[:4], refs[4], refs[5]
        for r in range(2):
            for s in range(4):

                @pl.when(plan_ref[6 + r] == s)
                def _(r=r, s=s):
                    pltpu.make_async_copy(ins[s], out.at[r], sems.at[r]).start()

        for r in range(2):
            pltpu.make_async_copy(ins[0], out.at[r], sems.at[r]).wait()

    return pl.pallas_call(
        body,
        out_shape=jax.ShapeDtypeStruct((2, count, rows, width), slots[0].dtype),
        in_specs=[SMEM] + [ANY] * 4,
        out_specs=ANY,
        scratch_shapes=[pltpu.SemaphoreType.DMA((2,))],
        name="far_return_pack",
    )(plan, *slots)


def head_unpack(plan, own_slots, sibling_slots, far, heads):
    count, rows, width = own_slots[0].shape

    def body(plan_ref, *refs):
        own, sib, far_ref = refs[:4], refs[4:8], refs[8]
        grads, attn, sems = refs[9], refs[10], refs[11]

        def target(t, i):
            columns = pl.ds(i * width, width)
            return grads.at[t, :, columns] if t < 3 else attn.at[:, columns]

        for i in range(heads):
            source = plan_ref[8 + i]
            for s in range(10):
                place = own[s] if s < 4 else sib[s - 4] if s < 8 else far_ref.at[s - 8]

                @pl.when(source == s)
                def _(i=i, place=place):
                    for t in range(count):
                        pltpu.make_async_copy(place.at[t], target(t, i), sems.at[i, t]).start()

        for i in range(heads):
            for t in range(count):
                pltpu.make_async_copy(own[0].at[t], target(t, i), sems.at[i, t]).wait()

    return pl.pallas_call(
        body,
        out_shape=[
            jax.ShapeDtypeStruct((3, rows, heads * width), own_slots[0].dtype),
            jax.ShapeDtypeStruct((rows, heads * width), own_slots[0].dtype),
        ],
        in_specs=[SMEM] + [ANY] * 9,
        out_specs=[ANY] * 2,
        scratch_shapes=[pltpu.SemaphoreType.DMA((heads, count))],
        name="head_unpack",
    )(plan, *own_slots, *sibling_slots, far)


def dot_nt(a, b):
    return lax.dot_general(a, b, (((1,), (1,)), ((), ())), preferred_element_type=F32)


def dot_nn(a, b):
    return lax.dot_general(a, b, (((1,), (0,)), ((), ())), preferred_element_type=F32)


def dot_tn(a, b):
    return lax.dot_general(a, b, (((0,), (0,)), ((), ())), preferred_element_type=F32)


def attend_body(
    block, plan_ref, me_ref, left, own, right, far, rank_l, rank_o, rank_r, rank_f, down,
    out_l, out_o, out_r, out_f,
    grad_rows, held, made, ranks, down_held, key_sum, value_sum, in_sems, rank_sems, out_sems,
):
    del grad_rows
    rows, width = own.shape[1], own.shape[2]
    total = 4 * rows
    factor = width**-0.5
    odd = lax.rem(me_ref[0], 2)
    starts = [(1 - odd) * rows, (2 - odd) * rows, (3 - odd) * rows, odd * 3 * rows]

    def at(i):
        return pl.ds(pl.multiple_of(starts[i], rows), rows)

    copies = []
    for i, source in enumerate((left, own, right, far)):
        copy = pltpu.make_async_copy(source, held.at[:, at(i)], in_sems.at[i])
        copy.start()
        copies.append(copy)
    for i, source in enumerate((rank_l, rank_o, rank_r, rank_f)):
        copy = pltpu.make_async_copy(source, ranks.at[at(i)], rank_sems.at[i])
        copy.start()
        copies.append(copy)
    copy = pltpu.make_async_copy(
        down.at[pl.ds(pl.multiple_of(plan_ref[13] * width, width), width)],
        down_held,
        rank_sems.at[4],
    )
    copy.start()
    copies.append(copy)
    key_sum[...] = jnp.zeros_like(key_sum)
    value_sum[...] = jnp.zeros_like(value_sum)
    for copy in copies:
        copy.wait()
    held[3] = (
        held[3].astype(F32) + adapter_scale * dot_nt(ranks[...], down_held[...])
    ).astype(BF16)
    mask = lax.broadcasted_iota(jnp.int32, (block, block), 1) <= lax.broadcasted_iota(
        jnp.int32, (block, block), 0
    )
    for i in reversed(range(total // block)):
        here = pl.ds(i * block, block)
        span = (i + 1) * block
        query, grad = held[0, here, :], held[3, here, :]
        keys, values = held[1, :span, :], held[2, :span, :]
        score = dot_nt(query, keys) * (factor * 1.4426950408889634)
        last = jnp.where(mask, score[:, i * block :], -1e30)
        score = jnp.concatenate([score[:, : i * block], last], axis=1) if i else last
        peak = jnp.max(score, axis=1, keepdims=True)
        weight = jnp.exp2(score - peak)
        attention = weight * (1.0 / jnp.sum(weight, axis=1, keepdims=True))
        attention_bf = attention.astype(BF16)
        out = dot_nn(attention_bf, values).astype(BF16)
        delta = jnp.sum(grad.astype(F32) * out.astype(F32), axis=1, keepdims=True)
        dscore = (attention * (dot_nt(grad, values) - delta)).astype(BF16)
        made[0, here, :] = (dot_nn(dscore, keys) * factor).astype(BF16)
        made[3, here, :] = out
        key_sum[:span, :] += dot_tn(dscore, query)
        value_sum[:span, :] += dot_tn(attention_bf, grad)
    made[1] = (key_sum[...] * factor).astype(BF16)
    made[2] = value_sum[...].astype(BF16)
    copies = []
    for i, target in enumerate((out_l, out_o, out_r, out_f)):
        copy = pltpu.make_async_copy(made.at[:, at(i)], target, out_sems.at[i])
        copy.start()
        copies.append(copy)
    for copy in copies:
        copy.wait()


def attend(plan, me, units, ranks, down, block=256):
    count, rows, width = units[0].shape
    total = 4 * rows
    rank = ranks[0].shape[1]
    return pl.pallas_call(
        functools.partial(attend_body, min(block, rows)),
        out_shape=[jax.ShapeDtypeStruct((4, rows, width), BF16)] * 4,
        in_specs=[SMEM, SMEM] + [ANY] * 9,
        out_specs=[ANY] * 4,
        scratch_shapes=[
            pltpu.VMEM((8, 128), F32),
            pltpu.VMEM((4, total, width), BF16),
            pltpu.VMEM((4, total, width), BF16),
            pltpu.VMEM((total, rank), BF16),
            pltpu.VMEM((width, rank), BF16),
            pltpu.VMEM((total, width), F32),
            pltpu.VMEM((total, width), F32),
            pltpu.SemaphoreType.DMA((4,)),
            pltpu.SemaphoreType.DMA((5,)),
            pltpu.SemaphoreType.DMA((4,)),
        ],
        compiler_params=pltpu.CompilerParams(vmem_limit_bytes=56 * 2**20),
        name="attend",
    )(plan, me, *units, *ranks, down)


def move(x, axis, target):
    count = lax.axis_size(axis)
    return lax.ppermute(x, axis, [(i, target(i) % count) for i in range(count)])


def up(x):
    return move(x, "ctx", lambda i: i + 1)


def down_one(x):
    return move(x, "ctx", lambda i: i - 1)


def cross(x):
    return move(x, "ctx", lambda i: i + 2 if i % 2 == 0 else i - 2)


def cross_back(x):
    return move(x, "ctx", lambda i: i - 2 if i % 2 == 0 else i + 2)


def sibling(x):
    return move(x, "head", lambda i: i ^ 1)


def far_exchange(case, x):
    def none(x):
        return x

    def one(x):
        return x.at[0].set(lax.ppermute(x[0], "head", [(1, 3), (3, 1)]))

    def two(x):
        return x.at[0].set(move(x[0], "head", lambda i: i ^ 2))

    def more(x):
        return move(x, "head", lambda i: i ^ 2)

    return lax.switch(case, (none, one, two, more), x)


def shards(
    inputs,
    queries,
    key_rows,
    value_rows,
    output_gradient,
    head_gradients,
    head_shift,
    down_qkv,
    up_qkv,
    output_down_adapter,
    up_out,
):
    rows_here, width = queries.shape
    heads_here = head_shift.shape[0]
    head_dim = width // heads_here
    place = lax.axis_index("ctx")
    column = lax.axis_index("head")
    me = jnp.stack([place, column]).astype(jnp.int32)
    shift_all = lax.all_gather(head_shift, "head", tiled=True)
    plan = make_plan(shift_all, place, column)
    case = plan[12]

    own = (queries, key_rows, value_rows, head_gradients)
    with jax.named_scope("heads_in"):
        sib = tuple(sibling(x) for x in own)
        far = far_exchange(case, far_pack(plan, own, head_dim))
        slots = slot_pack(plan, own, sib, far, head_dim)
        units = (up(slots[1]), slots[0], down_one(slots[2]), cross(slots[3]))

    with jax.named_scope("ranks_in"):
        output_part = jnp.einsum(
            "td,rd->tr", output_gradient, up_out, preferred_element_type=F32
        )
        input_part = jnp.einsum("td,kdr->ktr", inputs, down_qkv, preferred_element_type=F32)
        input_sum, output_sum = lax.psum((input_part, output_part), "head")
        input_lowrank = input_sum.astype(BF16)
        output_rank = output_sum.astype(BF16)
        ranks = (up(output_rank), output_rank, down_one(output_rank), cross(output_rank))
        down_all = lax.all_gather(output_down_adapter, "head", tiled=True)

    results = attend(plan, me, units, ranks, down_all)

    with jax.named_scope("heads_back"):
        back = (
            results[1],
            down_one(results[0]),
            up(results[2]),
            cross_back(results[3]),
        )
        back_sib = tuple(sibling(x) for x in back)
        back_far = far_exchange(case, far_return_pack(plan, back))
        projection_gradients, attention_result = head_unpack(
            plan, back, back_sib, back_far, heads_here
        )

    with jax.named_scope("adapters"):
        grad_part = jnp.einsum(
            "ktc,krc->ktr", projection_gradients, up_qkv, preferred_element_type=F32
        )
        out_part = jnp.einsum(
            "tc,cr->tr", attention_result, output_down_adapter, preferred_element_type=F32
        )
        grad_sum, out_sum = lax.psum((grad_part, out_part), "head")
        rank_gradient = grad_sum.astype(BF16)
        output_lowrank = out_sum.astype(BF16)
        projection_down = jnp.einsum(
            "nj,gnb->gjb", inputs, rank_gradient, preferred_element_type=F32
        )
        projection_up = jnp.einsum(
            "diy,dio->dyo", input_lowrank, projection_gradients, preferred_element_type=F32
        )
        output_down = jnp.einsum(
            "pu,pq->uq", attention_result, output_rank, preferred_element_type=F32
        )
        output_up = jnp.einsum(
            "qw,qj->wj", output_lowrank, output_gradient, preferred_element_type=F32
        )
        summed = lax.psum((projection_down, projection_up, output_down, output_up), "ctx")
        scale = adapter_scale * (rows_here * lax.axis_size("ctx")) ** (-0.5)
    return (projection_gradients, *(x * scale for x in summed))


def solution(mesh):
    placed = (
        P("ctx", "head"),
        P("ctx", "head"),
        P("ctx", "head"),
        P("ctx", "head"),
        P("ctx", "head"),
        P("ctx", "head"),
        P("head"),
        P(None, "head", None),
        P(None, None, "head"),
        P("head", None),
        P(None, "head"),
    )
    return jax.shard_map(
        shards,
        mesh=mesh,
        in_specs=placed,
        out_specs=(
            P(None, "ctx", "head"),
            P(None, "head", None),
            P(None, None, "head"),
            P("head", None),
            P(None, "head"),
        ),
        check_vma=False,
    )
```

time: 1170 us -> 948 us (0.81)
  waiting for transfers between devices: 602 us -> 327 us
  Pallas kernels: 0 us -> 152 us
  starting transfers between devices: 80.4 us -> 25.9 us
  matrix products: 33.8 us -> 7.21 us
  other arithmetic: 24.5 us -> 5.81 us
  blocking collectives: 393 us -> 410 us
  local copies, waits for them, and re-layouts: 17.7 us -> 4.56 us
    ppermute x20 -> x19, waiting for transfers between devices: 295 us -> 25 us  [the longest x17 25 us: move(): return lax.ppermute(x, axis, [(i, target(i) % count) for i in range(count)])]
    pallas_call x0 -> x6, Pallas kernels: none -> 152 us  [the longest x1 65.6 us: slot_pack(): pl.pallas_call(body, out_shape=[jax.ShapeDtypeStruct((count, rows, width)...]
    ppermute x20 -> x19, starting transfers between devices: 80.4 us -> 25.8 us  [the longest x17 24.5 us: move(): return lax.ppermute(x, axis, [(i, target(i) % count) for i in range(count)])]
    dot_general x29 -> x4, matrix products: 28.2 us -> 2.01 us  [the longest x1 0.97 us: shards(): jnp.einsum('nj,gnb->gjb', inputs, rank_gradient, preferred_element_type=F32)]
    psum x1, blocking collectives: 10.3 us -> 23 us  [shards(): input_sum, output_sum = lax.psum((input_part, output_part), 'head')]
  transfers between devices with their start and end apart: 21 -> 20, of which waited for: 15 -> 4; matrix products, arithmetic and copies ran while one was open for 2% -> 1% of each run, Pallas kernels for 0% -> 1%
where the time goes in v1:
time: 948 us
  blocking collectives  410 us (43%)
  waiting for transfers between devices  327 us (34%)
  Pallas kernels  152 us (16%)
  starting transfers between devices  25.9 us (3%)
  between operations  15.7 us (2%)
    psum x1, blocking collectives, shards(): lax.psum((projection_down, projection_up, output_down, output_up), 'ctx')  358 us
    psum x1, waiting for transfers between devices, shards(): lax.psum((projection_down, projection_up, output_down, output_up), 'ctx')  302 us
    pallas_call x1, Pallas kernels, slot_pack(): pl.pallas_call(body, out_shape=[jax.ShapeDtypeStruct((count, rows, width)...  65.6 us
    pallas_call x1, Pallas kernels, head_unpack(): pl.pallas_call(body, out_shape=[jax.ShapeDtypeStruct((3, rows, heads * wi...  65.5 us
    ppermute x17, waiting for transfers between devices, move(): return lax.ppermute(x, axis, [(i, target(i) % count) for i in range(count)])  25 us
    ppermute x17, starting transfers between devices, move(): return lax.ppermute(x, axis, [(i, target(i) % count) for i in range(count)])  24.5 us
    psum x1, blocking collectives, shards(): input_sum, output_sum = lax.psum((input_part, output_part), 'head')  23 us
  transfers between devices with their start and end apart: 20, of which 4 were waited for; matrix products, arithmetic and copies ran while one was open for 1% of the time, Pallas kernels for 1%

profile of v1, /device:TPU:8, one launch (start us, length us, event | category | flops | bytes accessed | tf_op | source)
XLA Modules:
  0.0 947.9 jit_solution(1373546349584230732)
XLA Ops:
  7.2 0.0 copy-start
  7.2 0.0 all-reduce.6.cloned.1.call-start
  7.2 0.1 collective-permute-start.6
  7.3 0.5 collective-permute-start.7
  7.8 0.1 collective-permute-start.8
  7.9 0.4 collective-permute-start.9
  8.3 1.3 dynamic-slice.32
  10.3 0.9 dynamic-update-slice.12
  11.1 6.1 all-reduce.shift_ref
  17.2 0.6 pad_add_fusion.me_ref
  17.8 1.4 plan.1.plan_ref
  19.2 1.2 slice.115
  20.4 2.0 far_pack.1
  23.1 0.9 conditional.2
  23.2 0.7 collective-permute-start.2
  23.9 0.1 bitcast_dynamic-update-slice_fusion
  24.0 0.0 copy-start.2
  24.0 0.0 copy-start.16
  24.0 0.0 collective-permute-done.8.refs_6_
  24.1 65.6 %slot_pack.1 = (bf16[4,512,128]{2,1,0:T(8,128)(2,1)}, bf16[4,512,128]{2,1,0:T(8,128)(2,1)}, bf16[4,512,128]{2,1,0:T(8,128)(2,1)}, bf16[4,512,128]{2,1,0:T(8,128)(2,1)}) custom-call(s32[16]{0:T(128)} %plan.1.plan_ref, bf16[512,512]{1,0:T(8,128)(2,1)} %refs_0_.3, bf16[512,512]{1,0:T(8,128)(2,1)} %refs_1_.3, bf16[512,512]{1,0:T(8,128)(2,1)} %refs_2_.3, ...), custom_call_target="tpu_custom_call" | custom-call | tf_op jit(solution)/shard_map/heads_in/slot_pack/pallas_call | solution.py:185
  89.7 0.0 copy-start.14
  89.7 0.7 collective-permute-start.10
  90.3 8.0 collective-permute-start.11
  98.3 0.0 collective-permute-start.12
  98.3 0.4 fusion.7
  98.7 23.0 %psum.56.rank_o = bf16[512,16]{1,0:T(8,128)(2,1)S(1)} all-reduce(f32[512,16]{1,0:T(8,128)S(1)} %fusion.7), channel_id=1, replica_groups=mesh['ctx'=64,'head'=4] {'head'}, use_global_device_ids=true, to_apply=%region_4.5 | all-reduce | flops 8192 | bytes 49152 | tf_op jit(solution)/shard_map/ranks_in/psum | solution.py:443
  121.8 0.1 collective-permute-start.13
  121.8 7.7 collective-permute-start.14
  129.6 0.1 copy.17
  129.7 3.4 collective-permute-done.13.rank_l
  133.1 7.1 all_gather.7.down
  140.2 4.5 collective-permute-done.15.rank_f
  144.7 0.6 copy-done.12
  145.3 0.2 copy-done.9
  145.5 15.5 %attend.1 = (bf16[4,512,128]{2,1,0:T(8,128)(2,1)}, bf16[4,512,128]{2,1,0:T(8,128)(2,1)}, bf16[4,512,128]{2,1,0:T(8,128)(2,1)}, bf16[4,512,128]{2,1,0:T(8,128)(2,1)}) custom-call(s32[16]{0:T(128)} %plan.1.plan_ref, s32[2]{0:T(128)} %pad_add_fusion.me_ref, bf16[4,512,128]{2,1,0:T(8,128)(2,1)} %copy-done.9, bf16[4,512,128]{2,1,0:T(8,128)(2,1)} %get-tuple-element.82.own, ...), custom_call_target="tpu_custom_call" | custom-call | tf_op jit(solution)/shard_map/attend/pallas_call | solution.py:345
  161.0 0.1 collective-permute-start.16
  161.1 2.0 collective-permute-start.17
  163.1 4.2 collective-permute-start.18
  167.3 17.2 %collective-permute-done.16.refs_1_ = bf16[4,512,128]{2,1,0:T(8,128)(2,1)S(1)} collective-permute-done((bf16[4,512,128]{2,1,0:T(8,128)(2,1)}, bf16[4,512,128]{2,1,0:T(8,128)(2,1)S(1)}, u32[]{:S(2)}, u32[]{:S(2)}) %collective-permute-start.16) | collective-permute-done | bytes 524320 | tf_op jit(solution)/shard_map/heads_back/ppermute | solution.py:369
  184.5 0.5 collective-permute-start.21
  185.0 0.1 collective-permute-start.22
  185.1 0.4 convolution_bitcast_fusion.1
  185.5 1.9 far_return_pack.1
  187.4 0.9 conditional.3
  187.5 0.7 collective-permute-start.4
  188.2 0.1 bitcast_dynamic-update-slice_fusion.2
  188.3 0.0 copy-start.15
  188.4 65.5 %head_unpack.1 = (bf16[3,512,512]{2,1,0:T(8,128)(2,1)}, bf16[512,512]{1,0:T(8,128)(2,1)}) custom-call(s32[16]{0:T(128)} %plan.1.plan_ref, bf16[4,512,128]{2,1,0:T(8,128)(2,1)} %get-tuple-element.85.refs_0_, bf16[4,512,128]{2,1,0:T(8,128)(2,1)} %copy-done.5, bf16[4,512,128]{2,1,0:T(8,128)(2,1)} %copy-done.6, ...), custom_call_target="tpu_custom_call" | custom-call | tf_op jit(solution)/shard_map/heads_back/head_unpack/pallas_call | solution.py:245
  253.8 0.0 copy-start.1
  253.8 1.4 fusion.10
  255.3 1.9 fusion.8
  257.2 15.4 %all-reduce.7 = (bf16[3,512,16]{1,2,0:T(8,128)(2,1)S(1)}, bf16[3,512,16]{1,2,0:T(8,128)(2,1)S(1)}, bf16[512,16]{1,0:T(8,128)(2,1)S(1)}) all-reduce(f32[3,512,16]{1,2,0:T(8,128)S(1)} %fusion.8, f32[3,512,16]{1,2,0:T(8,128)S(1)} %convolution_bitcast_fusion.1, f32[512,16]{1,0:T(8,128)S(1)} %fusion.10), channel_id=1, replica_groups=mesh['ctx'=64,'head'=4] {'head'}, use_global_device_ids=true, to_apply=%region_9.10 | all-reduce | flops 57344 | bytes 344064 | tf_op jit(solution)/shard_map/adapters/psum | solution.py:471
  272.6 0.0 copy-start.3
  272.6 1.0 fusion.12
  273.6 1.0 convolution_bitcast_fusion
  274.6 0.9 fusion.11
  275.5 0.0 all-reduce.6.cloned.1.call-update
  275.5 0.2 fusion.9
  275.7 358.1 %psum.61 = f32[512,16]{0,1:T(8,128)S(1)} all-reduce(f32[512,16]{0,1:T(8,128)S(1)} %fusion.9), channel_id=1, replica_groups=mesh['ctx'=64,'head'=4] {'ctx'}, use_global_device_ids=true, to_apply=%region_13.0 | all-reduce | flops 8192 | bytes 65536 | tf_op jit(solution)/shard_map/adapters/psum | solution.py:486
  633.9 0.6 broadcast_multiply_fusion.3
  634.5 301.9 %all-reduce.6.cloned.1.call-done = (f32[3,1024,16]{1,2,0:T(8,128)}, f32[3,16,512]{2,1,0:T(8,128)}, f32[16,1024]{1,0:T(8,128)}) async-done(((f32[3,1024,16]{1,2,0:T(8,128)}, f32[3,16,512]{2,1,0:T(8,128)}, f32[16,1024]{1,0:T(8,128)}), (f32[3,1024,16]{1,2,0:T(8,128)}, f32[3,16,512]{2,1,0:T(8,128)}, f32[16,1024]{1,0:T(8,128)})) %all-reduce.6.cloned.1.call-update) | async-done | bytes 360464 | tf_op jit(solution)/shard_map/adapters/psum | solution.py:486
  936.4 1.6 broadcast_multiply_fusion
  938.0 1.5 broadcast_multiply_fusion.1
  939.6 1.5 broadcast_multiply_fusion.2
  (46 shorter events, 0.2 us)
Async XLA Ops:
  7.2 177.9 %copy-start = (bf16[512,1024]{1,0:T(8,128)(2,1)S(1)}, bf16[512,1024]{1,0:T(8,128)(2,1)}, u32[]{:S(2)}) copy-start(bf16[512,1024]{1,0:T(8,128)(2,1)} %param.27) | copy-start | bytes 3145732
  7.2 929.2 %all-reduce.6.cloned.1.call-start = ((), (), s32[]{:S(2)}) async-start(), calls=%async_computation | async-start | bytes 720896 | tf_op jit(solution)/shard_map/adapters/psum | solution.py:486
  7.2 16.8 %collective-permute-start.6 = (bf16[512,512]{1,0:T(8,128)(2,1)}, bf16[512,512]{1,0:T(8,128)(2,1)}, u32[]{:S(2)}, u32[]{:S(2)}) collective-permute-start(bf16[512,512]{1,0:T(8,128)(2,1)} %refs_0_.3), channel_id=1, source_target_pairs={{0,1},{1,0},{2,3},{3,2},{4,5},{5,4},{6,7},{7,6},{8,9},{9,8},{10,11... | collective-permute-start | bytes 1572872 | tf_op jit(solution)/shard_map/heads_in/ppermute | solution.py:369
  7.3 16.7 %collective-permute-start.7 = (bf16[512,512]{1,0:T(8,128)(2,1)}, bf16[512,512]{1,0:T(8,128)(2,1)}, u32[]{:S(2)}, u32[]{:S(2)}) collective-permute-start(bf16[512,512]{1,0:T(8,128)(2,1)} %refs_1_.3), channel_id=1, source_target_pairs={{0,1},{1,0},{2,3},{3,2},{4,5},{5,4},{6,7},{7,6},{8,9},{9,8},{10,11... | collective-permute-start | bytes 1572872 | tf_op jit(solution)/shard_map/heads_in/ppermute | solution.py:369
  7.8 16.2 %collective-permute-start.8 = (bf16[512,512]{1,0:T(8,128)(2,1)}, bf16[512,512]{1,0:T(8,128)(2,1)}, u32[]{:S(2)}, u32[]{:S(2)}) collective-permute-start(bf16[512,512]{1,0:T(8,128)(2,1)} %refs_2_.3), channel_id=1, source_target_pairs={{0,1},{1,0},{2,3},{3,2},{4,5},{5,4},{6,7},{7,6},{8,9},{9,8},{10,11... | collective-permute-start | bytes 1572872 | tf_op jit(solution)/shard_map/heads_in/ppermute | solution.py:369
  7.9 16.1 %collective-permute-start.9 = (bf16[512,512]{1,0:T(8,128)(2,1)}, bf16[512,512]{1,0:T(8,128)(2,1)}, u32[]{:S(2)}, u32[]{:S(2)}) collective-permute-start(bf16[512,512]{1,0:T(8,128)(2,1)} %refs_3_.3), channel_id=1, source_target_pairs={{0,1},{1,0},{2,3},{3,2},{4,5},{5,4},{6,7},{7,6},{8,9},{9,8},{10,11... | collective-permute-start | bytes 1572872 | tf_op jit(solution)/shard_map/heads_in/ppermute | solution.py:369
  23.2 0.7 collective-permute-start.2
  24.0 74.3 %copy-start.2 = (bf16[512,1024]{1,0:T(8,128)(2,1)S(1)}, bf16[512,1024]{1,0:T(8,128)(2,1)}, u32[]{:S(2)}) copy-start(bf16[512,1024]{1,0:T(8,128)(2,1)} %param.31) | copy-start | bytes 3145732
  24.0 74.3 %copy-start.16 = (bf16[16,1024]{1,0:T(8,128)(2,1)S(1)}, bf16[16,1024]{1,0:T(8,128)(2,1)}, u32[]{:S(2)}) copy-start(bf16[16,1024]{1,0:T(8,128)(2,1)} %param.37) | copy-start | bytes 98308
  89.7 39.9 %copy-start.14 = (bf16[512,16]{0,1:T(8,128)(2,1)S(1)}, bf16[512,16]{0,1:T(8,128)(2,1)}, u32[]{:S(2)}) copy-start(bf16[512,16]{0,1:T(8,128)(2,1)} %param.36) | copy-start | bytes 49156
  89.7 55.0 %collective-permute-start.10 = (bf16[4,512,128]{2,1,0:T(8,128)(2,1)}, bf16[4,512,128]{2,1,0:T(8,128)(2,1)S(1)}, u32[]{:S(2)}, u32[]{:S(2)}) collective-permute-start(bf16[4,512,128]{2,1,0:T(8,128)(2,1)} %get-tuple-element.81), channel_id=1, source_target_pairs={{0,4},{4,8},{8,12},{12,16},{16,20},{20,24},{24,28},{28,32},{32,36}... | collective-permute-start | bytes 1572872 | tf_op jit(solution)/shard_map/heads_in/ppermute | solution.py:369
  90.3 54.3 %collective-permute-start.11 = (bf16[4,512,128]{2,1,0:T(8,128)(2,1)}, bf16[4,512,128]{2,1,0:T(8,128)(2,1)}, u32[]{:S(2)}, u32[]{:S(2)}) collective-permute-start(bf16[4,512,128]{2,1,0:T(8,128)(2,1)} %get-tuple-element.83), channel_id=1, source_target_pairs={{0,252},{4,0},{8,4},{12,8},{16,12},{20,16},{24,20},{28,24},{32,28}... | collective-permute-start | bytes 1572872 | tf_op jit(solution)/shard_map/heads_in/ppermute | solution.py:369
  98.3 46.4 %collective-permute-start.12 = (bf16[4,512,128]{2,1,0:T(8,128)(2,1)}, bf16[4,512,128]{2,1,0:T(8,128)(2,1)}, u32[]{:S(2)}, u32[]{:S(2)}) collective-permute-start(bf16[4,512,128]{2,1,0:T(8,128)(2,1)} %get-tuple-element.84), channel_id=1, source_target_pairs={{0,8},{4,252},{8,16},{12,4},{16,24},{20,12},{24,32},{28,20},{32,40... | collective-permute-start | bytes 1572872 | tf_op jit(solution)/shard_map/heads_in/ppermute | solution.py:369
  121.7 22.9 %copy-start.7 = (bf16[512,16]{1,0:T(8,128)(2,1)}, bf16[512,16]{1,0:T(8,128)(2,1)S(1)}, u32[]{:S(2)}) copy-start(bf16[512,16]{1,0:T(8,128)(2,1)S(1)} %psum.56.rank_o) | copy-start | bytes 49156
  121.8 11.3 %collective-permute-start.13 = (bf16[512,16]{1,0:T(8,128)(2,1)S(1)}, bf16[512,16]{1,0:T(8,128)(2,1)S(1)}, u32[]{:S(2)}, u32[]{:S(2)}) collective-permute-start(bf16[512,16]{1,0:T(8,128)(2,1)S(1)} %psum.56.rank_o), channel_id=1, source_target_pairs={{0,4},{4,8},{8,12},{12,16},{16,20},{20,24},{24,28},{28,32},{32,36}... | collective-permute-start | bytes 49160 | tf_op jit(solution)/shard_map/ranks_in/ppermute | solution.py:369
  121.8 18.4 %collective-permute-start.14 = (bf16[512,16]{1,0:T(8,128)(2,1)S(1)}, bf16[512,16]{1,0:T(8,128)(2,1)S(1)}, u32[]{:S(2)}, u32[]{:S(2)}) collective-permute-start(bf16[512,16]{1,0:T(8,128)(2,1)S(1)} %psum.56.rank_o), channel_id=1, source_target_pairs={{0,252},{4,0},{8,4},{12,8},{16,12},{20,16},{24,20},{28,24},{32,28}... | collective-permute-start | bytes 49160 | tf_op jit(solution)/shard_map/ranks_in/ppermute | solution.py:369
  133.1 11.6 %copy-start.10 = (bf16[512,16]{1,0:T(8,128)(2,1)}, bf16[512,16]{1,0:T(8,128)(2,1)S(1)}, u32[]{:S(2)}) copy-start(bf16[512,16]{1,0:T(8,128)(2,1)S(1)} %collective-permute-done.13.rank_l) | copy-start | bytes 49156
  133.1 11.6 %collective-permute-start.15 = (bf16[512,16]{1,0:T(8,128)(2,1)S(1)}, bf16[512,16]{1,0:T(8,128)(2,1)S(1)}, u32[]{:S(2)}, u32[]{:S(2)}) collective-permute-start(bf16[512,16]{1,0:T(8,128)(2,1)S(1)} %psum.56.rank_o), channel_id=1, source_target_pairs={{0,8},{4,252},{8,16},{12,4},{16,24},{20,12},{24,32},{28,20},{32,40... | collective-permute-start | bytes 49160 | tf_op jit(solution)/shard_map/ranks_in/ppermute | solution.py:369
  140.2 4.5 copy-start.11
  144.7 0.7 copy-start.12
  144.7 0.8 copy-start.9
  145.5 39.6 %copy-start.13 = (bf16[3,1024,16]{1,2,0:T(8,128)(2,1)S(1)}, bf16[3,1024,16]{1,2,0:T(8,128)(2,1)}, u32[]{:S(2)}) copy-start(bf16[3,1024,16]{1,2,0:T(8,128)(2,1)} %param.34) | copy-start | bytes 294916
  161.0 23.5 %collective-permute-start.16 = (bf16[4,512,128]{2,1,0:T(8,128)(2,1)}, bf16[4,512,128]{2,1,0:T(8,128)(2,1)S(1)}, u32[]{:S(2)}, u32[]{:S(2)}) collective-permute-start(bf16[4,512,128]{2,1,0:T(8,128)(2,1)} %get-tuple-element.86), channel_id=1, source_target_pairs={{0,252},{4,0},{8,4},{12,8},{16,12},{20,16},{24,20},{28,24},{32,28}... | collective-permute-start | bytes 1572872 | tf_op jit(solution)/shard_map/heads_back/ppermute | solution.py:369
  161.1 23.3 %collective-permute-start.17 = (bf16[4,512,128]{2,1,0:T(8,128)(2,1)}, bf16[4,512,128]{2,1,0:T(8,128)(2,1)S(1)}, u32[]{:S(2)}, u32[]{:S(2)}) collective-permute-start(bf16[4,512,128]{2,1,0:T(8,128)(2,1)} %get-tuple-element.87), channel_id=1, source_target_pairs={{0,4},{4,8},{8,12},{12,16},{16,20},{20,24},{24,28},{28,32},{32,36}... | collective-permute-start | bytes 1572872 | tf_op jit(solution)/shard_map/heads_back/ppermute | solution.py:369
  163.1 21.9 %collective-permute-start.18 = (bf16[4,512,128]{2,1,0:T(8,128)(2,1)}, bf16[4,512,128]{2,1,0:T(8,128)(2,1)}, u32[]{:S(2)}, u32[]{:S(2)}) collective-permute-start(bf16[4,512,128]{2,1,0:T(8,128)(2,1)} %get-tuple-element.88), channel_id=1, source_target_pairs={{0,248},{4,12},{8,0},{12,20},{16,8},{20,28},{24,16},{28,36},{32,24... | collective-permute-start | bytes 1572872 | tf_op jit(solution)/shard_map/heads_back/ppermute | solution.py:369
  167.3 21.0 %collective-permute-start.19 = (bf16[4,512,128]{2,1,0:T(8,128)(2,1)}, bf16[4,512,128]{2,1,0:T(8,128)(2,1)}, u32[]{:S(2)}, u32[]{:S(2)}) collective-permute-start(bf16[4,512,128]{2,1,0:T(8,128)(2,1)} %get-tuple-element.85.refs_0_), channel_id=1, source_target_pairs={{0,1},{1,0},{2,3},{3,2},{4,5},{5,4},{6,7},{7,6},{8,9},{9,8},{10,11... | collective-permute-start | bytes 1572872 | tf_op jit(solution)/shard_map/heads_back/ppermute | solution.py:369
  184.5 1.1 copy-start.5
  184.5 3.9 collective-permute-start.20
  184.5 1.1 copy-start.6
  184.5 3.9 collective-permute-start.21
  185.0 3.4 collective-permute-start.22
  187.5 0.7 collective-permute-start.4
  188.3 67.0 %copy-start.15 = (bf16[3,16,512]{2,1,0:T(8,128)(2,1)S(1)}, bf16[3,16,512]{2,1,0:T(8,128)(2,1)}, u32[]{:S(2)}) copy-start(bf16[3,16,512]{2,1,0:T(8,128)(2,1)} %param.35) | copy-start | bytes 147460
  253.8 18.8 %copy-start.1 = (bf16[3,512,512]{2,1,0:T(8,128)(2,1)S(1)}, bf16[3,512,512]{2,1,0:T(8,128)(2,1)}, u32[]{:S(2)}) copy-start(bf16[3,512,512]{2,1,0:T(8,128)(2,1)} %get-tuple-element.76) | copy-start | bytes 4718596
  272.6 2.0 copy-start.3
  273.6 1.9 copy-start.4
  273.6 1.9 copy-start.8
Sparse Core Ops, SparseCore 0:
  275.6 660.7 all-reduce.5
